TPU v7x, 128 devices: a whole 4x4x4 slice. The times are simulated.
128 devices in a mesh: branch: 32 (over x, z, core), sub: 4 (over y).
Axes of the slice: x: 4, y: 4, z: 4, core: 2. Of those that a mesh axis runs over, the one named last changes fastest.
Arguments:
- right_sides: bfloat16 [32, 786432], P(None, ('branch', 'sub')), may hold values from -6 to 6
- near_blocks: bfloat16 [3072, 6, 256, 256], P(('branch', 'sub')), may hold values from -0.15625 to 0.15625
- near_list: int32 [3072, 6], P(('branch', 'sub')), may hold values from -1 to 3071, as said below
- leaf_basis: bfloat16 [3072, 64, 256], P(('branch', 'sub')), may hold values from -0.375 to 0.375
- leaf_parent: int32 [128, 24], P(('branch', 'sub')), may hold values from 0 to 5, never falling along the last dimension, each value on 1 to 6 neighbouring positions
- leaf_upward_matrix: float32 [3072, 64, 64], P(('branch', 'sub')), may hold values from -0.375 to 0.375
- mid_pairs: int32 [768, 4], P(('branch', 'sub')), may hold values from -1 to 767, as said below
- mid_coupling: float32 [768, 4, 64, 64], P(('branch', 'sub')), may hold values from -0.75 to 0.75
- mid_transfer: float32 [768, 64, 64], P(('branch', 'sub')), may hold values from -0.3125 to 0.3125
- node_pairs: int32 [128, 8], P('branch'), may hold values from -1 to 127, as said below
- node_coupling: float32 [128, 8, 64, 64], P('branch'), may hold values from -0.5 to 0.5
- node_transfer: float32 [128, 64, 64], P('branch'), may hold values from -0.375 to 0.375
- branch_pairs: int32 [32, 4], P('branch'), may hold values from -1 to 31, as said below
- branch_coupling: float32 [32, 4, 64, 64], P('branch'), may hold values from -1.5 to 1.5
Outputs:
- product: float32 [32, 786432], P(None, ('branch', 'sub'))
Inputs may be any that keep to these rules, and one draw needn't show every extreme that they name: `near_list`: entry (l, 0) is l itself; every other entry is -1 or a leaf j != l with |j - l| <= 24; the leaves of a row are distinct. `leaf_parent`: within a row the parent never falls, and every parent has 1 to 6 leaves. `mid_pairs`: every entry is -1 or a level-1 cluster j != q with |j - q| <= 6; the clusters of a row are distinct. `node_pairs`: every entry is -1 or a node other than the row's own; the nodes of a row are distinct; entry (p, 0) is never -1. `branch_pairs`: every entry is -1 or a branch other than the row's own; the branches of a row are distinct; entry (b, 0) is never -1.
All inputs are finite; a program needn't handle non-finite values.
Results may differ from a plain program's by a relative error of at most 0.0003.
Values may be sent and summed in bfloat16 or wider, within the bound.
A program may use at most 128 MiB of HBM per device.

v0:
```python
import jax
import jax.numpy as jnp
from jax import lax
from jax.sharding import PartitionSpec as P

highest_accuracy = lax.Precision.HIGHEST


def with_halo(cells, sides, width):
    for axis, dim in sides:
        count = lax.axis_size(axis)
        ends = count - 1
        head = lax.slice_in_dim(cells, 0, width, axis=dim)
        tail = lax.slice_in_dim(cells, cells.shape[dim] - width, cells.shape[dim], axis=dim)
        cells = jnp.concatenate(
            [
                lax.ppermute(tail, axis, [(i, (i + 1) % count) for i in range(ends)]),
                cells,
                lax.ppermute(head, axis, [((i + 1) % count, i) for i in range(ends)]),
            ],
            axis=dim,
        )
    return cells


def masked_rows(source, indices):
    present = indices >= 0
    clipped = jnp.where(present, indices, 0)
    taken = source[clipped]
    out_shape = present.shape + (1,) * (taken.ndim - present.ndim)
    return jnp.where(present.reshape(out_shape), taken, jnp.zeros((), taken.dtype))


def on_device(
    right_sides,
    near_blocks,
    near_list,
    leaf_basis,
    leaf_parent,
    leaf_upward_matrix,
    mid_pairs,
    mid_coupling,
    mid_transfer,
    node_pairs,
    node_coupling,
    node_transfer,
    branch_pairs,
    branch_coupling,
):
    rhs_count, columns = right_sides.shape
    leaf_count, basis_rank, leaf_size = leaf_basis.shape
    clusters = mid_pairs.shape[0]
    sub_count = lax.axis_size("sub")
    sub_at = lax.axis_index("sub")
    node_at = lax.axis_index("branch") * sub_count + sub_at
    window = with_halo(right_sides, ((("branch", "sub"), 1),), columns)
    window_leaves = window.reshape(rhs_count, 3 * leaf_count, leaf_size)
    present = near_list >= 0
    slot_index = jnp.where(present, near_list - (node_at * leaf_count - leaf_count), 0)
    picked = jnp.take(window_leaves, slot_index, axis=1)
    picked = jnp.where(present[None, :, :, None], picked, jnp.zeros((), picked.dtype))
    near_part = jnp.einsum(
        "ikab,nikb->nia", near_blocks, picked, preferred_element_type=jnp.float32
    )
    leaf_coefficients = jnp.einsum(
        "nlk,lrk->lnr",
        right_sides.reshape(rhs_count, leaf_count, leaf_size),
        leaf_basis,
        preferred_element_type=jnp.float32,
    )
    member = (leaf_parent[0][:, None] == jnp.arange(clusters, dtype=jnp.int32)[None, :]).astype(
        jnp.float32
    )
    raised_coefficients = jnp.einsum(
        "xvm,xmu->xvu", leaf_coefficients, leaf_upward_matrix, precision=highest_accuracy
    )
    coef_mid = jnp.einsum("lq,lnr->qnr", member, raised_coefficients, precision=highest_accuracy)
    coef_node = jnp.einsum("qns,qsr->nr", coef_mid, mid_transfer, precision=highest_accuracy)
    own_transfer = lax.dynamic_index_in_dim(node_transfer, sub_at, 0, keepdims=False)
    top_term = jnp.einsum("ns,sr->nr", coef_node, own_transfer, precision=highest_accuracy)
    mid_window = with_halo(coef_mid, ((("branch", "sub"), 0),), clusters)
    mid_present = mid_pairs >= 0
    mid_index = jnp.where(mid_present, mid_pairs - (node_at * clusters - clusters), -1)
    middle_potential = jnp.einsum(
        "qkrs,qkns->qnr",
        mid_coupling,
        masked_rows(mid_window, mid_index),
        precision=highest_accuracy,
    )
    all_coef, all_terms = (
        lax.all_gather(coef_node[None], ("branch", "sub"), axis=0, tiled=True),
        lax.all_gather(top_term[None], ("branch", "sub"), axis=0, tiled=True),
    )
    branches = all_terms.shape[0] // sub_count
    coef_branch = all_terms.reshape(branches, sub_count, rhs_count, basis_rank).sum(axis=1)
    field_branch = jnp.einsum(
        "krs,kns->nr",
        branch_coupling[0],
        masked_rows(coef_branch, branch_pairs[0]),
        precision=highest_accuracy,
    )
    own_pairs = lax.dynamic_index_in_dim(node_pairs, sub_at, 0, keepdims=False)
    own_coupling = lax.dynamic_index_in_dim(node_coupling, sub_at, 0, keepdims=False)
    field_node = jnp.einsum(
        "krs,kns->nr", own_coupling, masked_rows(all_coef, own_pairs), precision=highest_accuracy
    )
    field_node = field_node + jnp.einsum(
        "sr,nr->ns", own_transfer, field_branch, precision=highest_accuracy
    )
    middle_potential = middle_potential + jnp.einsum(
        "qsr,nr->qns", mid_transfer, field_node, precision=highest_accuracy
    )
    broadcast_down = jnp.einsum("lq,qnr->lnr", member, middle_potential, precision=highest_accuracy)
    leaf_potential = jnp.einsum(
        "vpt,vct->vcp", leaf_upward_matrix, broadcast_down, precision=highest_accuracy
    )
    far_part = jnp.einsum(
        "lrk,lnr->nlk", leaf_basis.astype(jnp.float32), leaf_potential, precision=highest_accuracy
    )
    return near_part.reshape(rhs_count, columns) + far_part.reshape(rhs_count, columns)


def solution(mesh):
    return jax.shard_map(
        on_device,
        mesh=mesh,
        in_specs=(
            P(None, ("branch", "sub")),
            P(("branch", "sub"), None, None, None),
            P(("branch", "sub"), None),
            P(("branch", "sub"), None, None),
            P(("branch", "sub"), None),
            P(("branch", "sub"), None, None),
            P(("branch", "sub"), None),
            P(("branch", "sub"), None, None, None),
            P(("branch", "sub"), None, None),
            P("branch", None),
            P("branch", None, None, None),
            P("branch", None, None),
            P("branch", None),
            P("branch", None, None, None),
        ),
        out_specs=P(None, ("branch", "sub")),
        check_vma=False,
    )
```

profile of v0, /device:TPU:0, one launch (start us, length us, event | category | flops | bytes accessed | tf_op | source)
XLA Modules:
  0.0 166.7 jit_solution(2003805883413682369)
XLA Ops:
  6.5 0.0 copy-start
  6.5 0.0 copy-start.4
  6.5 0.0 copy-start.9
  6.5 0.0 copy-start.11
  6.6 0.0 copy-start.8
  6.6 0.0 copy-start.10
  6.6 0.0 all-gather.5.cloned.1.call-start
  6.6 1.7 %fusion.14 = f32[24,32,64]{2,1,0:T(8,128)S(1)} fusion(bf16[24,64,256]{2,1,0:T(8,128)(2,1)} %param.17, bf16[4,24,8,256]{3,2,1,0:T(8,128)(2,1)} %bitcast.84), kind=kOutput, calls=%fused_computation.25 | convolution fusion | flops 25165824 | bytes 1376256 | tf_op jit(solution)/shard_map/nlk,lrk->lnr/dot_general | solution.py:65
  8.3 2.0 %fusion.57 = f32[24,32,64]{2,1,0:T(8,128)S(1)} fusion(f32[24,32,64]{2,1,0:T(8,128)S(1)} %fusion.14, f32[24,64,64]{2,1,0:T(8,128)} %param.19), kind=kOutput, calls=%fused_computation.84 | convolution fusion | flops 37748736 | bytes 786432 | tf_op jit(solution)/shard_map/xvm,xmu->xvu/dot_general | solution.py:74
  10.3 0.0 copy-done.9
  10.4 0.5 fusion.19
  10.8 0.0 copy-done.6
  10.8 0.9 convolution_bitcast_fusion.3
  11.7 0.0 all-gather.5.cloned.1.call-update
  11.8 0.0 all-gather.7.cloned.1.call-start
  11.8 0.0 copy-done.4
  11.8 1.3 collective-permute-start.1
  13.1 5.3 %collective-permute-start = (bf16[32,6144]{1,0:T(8,128)(2,1)S(1)}, bf16[32,6144]{1,0:T(8,128)(2,1)}, u32[]{:S(2)}, u32[]{:S(2)}) collective-permute-start(bf16[32,6144]{1,0:T(8,128)(2,1)S(1)} %copy-done.4), channel_id=1, source_target_pairs={{0,1},{1,2},{2,3},{3,4},{4,5},{5,6},{6,7},{7,8},{8,9},{9,10},{10,1... | collective-permute-start | bytes 1179656 | tf_op jit(solution)/shard_map/ppermute | solution.py:17
  18.4 1.3 collective-permute-start.3
  19.7 4.6 %collective-permute-start.2 = (f32[6,32,64]{2,0,1:T(8,128)S(1)}, f32[6,32,64]{2,0,1:T(8,128)S(1)}, u32[]{:S(2)}, u32[]{:S(2)}) collective-permute-start(f32[6,32,64]{2,0,1:T(8,128)S(1)} %fusion.19), channel_id=1, source_target_pairs={{0,1},{1,2},{2,3},{3,4},{4,5},{5,6},{6,7},{7,8},{8,9},{9,10},{10,1... | collective-permute-start | bytes 147464 | tf_op jit(solution)/shard_map/ppermute | solution.py:17
  24.3 1.5 fusion.35
  25.8 0.0 all-gather.7.cloned.1.call-update
  25.8 0.0 copy-done.7
  25.9 0.0 copy-done.11
  25.9 0.0 copy-done.8
  25.9 0.1 copy.31
  26.0 0.1 reshape.98
  26.1 0.1 copy.36
  26.2 0.1 reshape.106
  26.3 0.0 copy-done.10
  26.4 0.5 compare_bitcast_fusion.1
  26.9 0.1 copy.29
  27.0 0.1 copy.30
  27.1 0.1 copy.33
  27.2 0.1 collective-permute-done.3
  27.3 2.3 %collective-permute-done.2 = f32[6,32,64]{2,0,1:T(8,128)S(1)} collective-permute-done((f32[6,32,64]{2,0,1:T(8,128)S(1)}, f32[6,32,64]{2,0,1:T(8,128)S(1)}, u32[]{:S(2)}, u32[]{:S(2)}) %collective-permute-start.2) | collective-permute-done | bytes 49184 | tf_op jit(solution)/shard_map/ppermute | solution.py:17
  29.6 0.1 pad_maximum_fusion.1
  29.7 0.1 copy.37
  29.7 0.6 gather_fusion.1
  30.3 0.0 copy-done.5
  30.3 1.5 convolution_bitcast_fusion.1
  31.8 0.0 collective-permute-done.1
  31.8 0.0 collective-permute-done
  31.8 1.1 pad_maximum_fusion
  32.9 1.2 copy.60
  34.1 2.1 %gather_fusion = bf16[144,32,256]{2,1,0:T(8,128)(2,1)S(1)} fusion(bf16[32,72,256]{2,0,1:T(8,128)(2,1)} %bitcast.81, s32[1024]{0:T(1024)S(1)} %pad_clamp_fusion.3), kind=kCustom, calls=%fused_computation | custom fusion | bytes 4719168 | tf_op jit(solution)/shard_map/jit(_take)/gather | solution.py:60
  36.2 10.3 %fusion.6 = f32[24,32,256]{2,1,0:T(8,128)} fusion(bf16[24,6,256,256]{3,2,1,0:T(8,128)(2,1)} %param.15, bf16[24,6,32,256]{3,2,1,0:T(8,128)(2,1)S(1)} %bitcast.80, pred[24,6]{1,0:T(8,128)(4,1)S(1)} %copy.29, pred[24,6]{1,0:T(8,128)(4,1)S(1)} %copy.30), kind=kOutput, calls=%fused_computation.10 | convolution fusion | flops 606339072 | bytes 22020384 | tf_op jit(solution)/shard_map/ikab,nikb->nia/dot_general | solution.py:62
  46.5 34.7 %all-gather.5.cloned.1.call-done = f32[4096,64]{1,0:T(8,128)} async-done(((f32[32,64]{1,0:T(8,128)}), f32[4096,64]{1,0:T(8,128)}) %all-gather.5.cloned.1.call-update) | async-done | bytes 1048592 | tf_op jit(solution)/shard_map/all_gather | solution.py:91
  81.2 2.1 %gather_fusion.2 = f32[8,32,64]{2,1,0:T(8,128)S(1)} fusion(f32[128,32,64]{2,1,0:T(8,128)} %bitcast.86, s32[1024]{0:T(1024)S(1)} %pad_clamp_fusion.1), kind=kCustom, calls=%fused_computation.2 | custom fusion | bytes 131104 | tf_op jit(solution)/shard_map/gather | solution.py:29
  83.3 63.5 %all-gather.7.cloned.1.call-done = f32[4096,64]{1,0:T(8,128)} async-done(((f32[32,64]{1,0:T(8,128)}), f32[4096,64]{1,0:T(8,128)}) %all-gather.7.cloned.1.call-update) | async-done | bytes 1048592 | tf_op jit(solution)/shard_map/all_gather | solution.py:92
  146.9 2.8 %reduce_sum.9 = f32[32,32,64]{2,1,0:T(8,128)} reduce(f32[32,4,32,64]{3,2,1,0:T(8,128)} %bitcast.83, f32[]{:T(128)} %constant.61.clone.1), dimensions={1}, to_apply=%region_0.1 | reduce | flops 196608 | bytes 1310724 | tf_op jit(solution)/shard_map/reduce_sum | solution.py:95
  149.7 2.2 %gather_fusion.3 = f32[4,32,64]{2,1,0:T(8,128)} fusion(f32[32,32,64]{2,1,0:T(8,128)} %reduce_sum.9, s32[1024]{0:T(1024)S(1)} %pad_clamp_fusion), kind=kCustom, calls=%fused_computation.3 | custom fusion | bytes 65552 | tf_op jit(solution)/shard_map/gather | solution.py:29
  151.9 0.0 copy-done
  151.9 1.0 convolution_bitcast_fusion.4
  152.9 1.2 convolution_bitcast_fusion.2
  154.1 0.9 fusion.13
  155.1 1.6 fusion.12
  156.7 0.4 fusion.27
  157.1 0.0 copy-done.1
  157.1 1.3 fusion.17
  158.5 0.0 copy-done.2
  158.5 0.0 copy-done.3
  158.5 0.5 fusion.9
  158.9 1.0 copy.46
  (16 shorter events, 0.1 us)
Async XLA Ops:
  6.5 145.4 %copy-start = (f32[4,8,64,64]{3,2,1,0:T(8,128)S(1)}, f32[4,8,64,64]{3,2,1,0:T(8,128)}, u32[]{:S(2)}) copy-start(f32[4,8,64,64]{3,2,1,0:T(8,128)} %param.24) | copy-start | bytes 1572868
  6.5 5.3 %copy-start.4 = (bf16[32,6144]{1,0:T(8,128)(2,1)S(1)}, bf16[32,6144]{1,0:T(8,128)(2,1)}, u32[]{:S(2)}) copy-start(bf16[32,6144]{1,0:T(8,128)(2,1)} %param.14) | copy-start | bytes 1179652
  6.5 3.8 %copy-start.9 = (s32[1,24]{1,0:T(1,128)S(1)}, s32[1,24]{1,0:T(1,128)}, u32[]{:S(2)}) copy-start(s32[1,24]{1,0:T(1,128)} %param.18) | copy-start | bytes 292
  6.5 4.3 %copy-start.6 = (f32[6,64,64]{2,1,0:T(8,128)S(1)}, f32[6,64,64]{2,1,0:T(8,128)}, u32[]{:S(2)}) copy-start(f32[6,64,64]{2,1,0:T(8,128)} %param.22) | copy-start | bytes 294916
  6.5 19.3 %copy-start.7 = (s32[6,4]{0,1:T(4,128)S(1)}, s32[6,4]{0,1:T(4,128)}, u32[]{:S(2)}) copy-start(s32[6,4]{0,1:T(4,128)} %param.20) | copy-start | bytes 292
  6.5 19.3 %copy-start.11 = (s32[1,4]{1,0:T(1,128)S(1)}, s32[1,4]{1,0:T(1,128)}, u32[]{:S(2)}) copy-start(s32[1,4]{1,0:T(1,128)} %param.26) | copy-start | bytes 52
  6.6 19.4 %copy-start.8 = (s32[24,6]{0,1:T(8,128)S(1)}, s32[24,6]{0,1:T(8,128)}, u32[]{:S(2)}) copy-start(s32[24,6]{0,1:T(8,128)} %param.16) | copy-start | bytes 1732
  6.6 19.8 %copy-start.10 = (s32[4,8]{1,0:T(4,128)S(1)}, s32[4,8]{1,0:T(4,128)}, u32[]{:S(2)}) copy-start(s32[4,8]{1,0:T(4,128)} %param.23) | copy-start | bytes 388
  6.6 74.6 %all-gather.5.cloned.1.call-start = ((), (), s32[]{:S(2)}) async-start(), calls=%async_computation | async-start | bytes 2113536 | tf_op jit(solution)/shard_map/all_gather | solution.py:91
  8.3 22.0 %copy-start.5 = (f32[6,4,64,64]{3,2,1,0:T(8,128)S(1)}, f32[6,4,64,64]{3,2,1,0:T(8,128)}, u32[]{:S(2)}) copy-start(f32[6,4,64,64]{3,2,1,0:T(8,128)} %param.21) | copy-start | bytes 1179652
  11.8 135.1 %all-gather.7.cloned.1.call-start = ((), (), s32[]{:S(2)}) async-start(), calls=%async_computation.1 | async-start | bytes 2113536 | tf_op jit(solution)/shard_map/all_gather | solution.py:92
  11.8 20.0 %collective-permute-start.1 = (bf16[32,6144]{1,0:T(8,128)(2,1)S(1)}, bf16[32,6144]{1,0:T(8,128)(2,1)S(1)}, u32[]{:S(2)}, u32[]{:S(2)}) collective-permute-start(bf16[32,6144]{1,0:T(8,128)(2,1)S(1)} %copy-done.4), channel_id=1, source_target_pairs={{1,0},{2,1},{3,2},{4,3},{5,4},{6,5},{7,6},{8,7},{9,8},{10,9},{11,1... | collective-permute-start | bytes 1179656 | tf_op jit(solution)/shard_map/ppermute | solution.py:19
  13.1 18.7 %collective-permute-start = (bf16[32,6144]{1,0:T(8,128)(2,1)S(1)}, bf16[32,6144]{1,0:T(8,128)(2,1)}, u32[]{:S(2)}, u32[]{:S(2)}) collective-permute-start(bf16[32,6144]{1,0:T(8,128)(2,1)S(1)} %copy-done.4), channel_id=1, source_target_pairs={{0,1},{1,2},{2,3},{3,4},{4,5},{5,6},{6,7},{7,8},{8,9},{9,10},{10,1... | collective-permute-start | bytes 1179656 | tf_op jit(solution)/shard_map/ppermute | solution.py:17
  18.4 8.9 %collective-permute-start.3 = (f32[6,32,64]{2,0,1:T(8,128)S(1)}, f32[6,32,64]{2,0,1:T(8,128)S(1)}, u32[]{:S(2)}, u32[]{:S(2)}) collective-permute-start(f32[6,32,64]{2,0,1:T(8,128)S(1)} %fusion.19), channel_id=1, source_target_pairs={{1,0},{2,1},{3,2},{4,3},{5,4},{6,5},{7,6},{8,7},{9,8},{10,9},{11,1... | collective-permute-start | bytes 147464 | tf_op jit(solution)/shard_map/ppermute | solution.py:19
  19.7 9.9 %collective-permute-start.2 = (f32[6,32,64]{2,0,1:T(8,128)S(1)}, f32[6,32,64]{2,0,1:T(8,128)S(1)}, u32[]{:S(2)}, u32[]{:S(2)}) collective-permute-start(f32[6,32,64]{2,0,1:T(8,128)S(1)} %fusion.19), channel_id=1, source_target_pairs={{0,1},{1,2},{2,3},{3,4},{4,5},{5,6},{6,7},{7,8},{8,9},{9,10},{10,1... | collective-permute-start | bytes 147464 | tf_op jit(solution)/shard_map/ppermute | solution.py:17
  46.5 110.6 %copy-start.1 = (f32[24,64,64]{2,1,0:T(8,128)S(1)}, f32[24,64,64]{2,1,0:T(8,128)}, u32[]{:S(2)}) copy-start(f32[24,64,64]{2,1,0:T(8,128)} %param.19) | copy-start | bytes 1179652
  146.9 11.6 %copy-start.2 = (bf16[24,64,256]{2,1,0:T(8,128)(2,1)S(1)}, bf16[24,64,256]{2,1,0:T(8,128)(2,1)}, u32[]{:S(2)}) copy-start(bf16[24,64,256]{2,1,0:T(8,128)(2,1)} %param.17) | copy-start | bytes 2359300
  146.9 11.6 %copy-start.3 = (f32[24,32,256]{2,1,0:T(8,128)S(1)}, f32[24,32,256]{2,1,0:T(8,128)}, u32[]{:S(2)}) copy-start(f32[24,32,256]{2,1,0:T(8,128)} %fusion.6) | copy-start | bytes 2359300
Sparse Core Ops, SparseCore 0:
  11.9 69.2 all-gather.4
  84.2 62.6 all-gather.6
where the time goes:
time: 168 us; the launch traced here: 167 us
  waiting for transfers between devices  101 us (60%)
  matrix products  25.4 us (15%)
  between operations  13.7 us (8%)
  starting transfers between devices  12.5 us (7%)
  local copies, waits for them, and re-layouts  9.93 us (6%)
  other arithmetic  4.57 us (3%)
    all_gather x1, waiting for transfers between devices, on_device(): lax.all_gather(top_term[None], ('branch', 'sub'), axis=0, tiled=True)  63.5 us
    all_gather x1, waiting for transfers between devices, on_device(): lax.all_gather(coef_node[None], ('branch', 'sub'), axis=0, tiled=True)  34.7 us
    dot_general x1, matrix products, on_device(): jnp.einsum('ikab,nikb->nia', near_blocks, picked, preferred_element_type=...  10.3 us
    ppermute x2, starting transfers between devices, with_halo(): lax.ppermute(tail, axis, [(i, (i + 1) % count) for i in range(ends)])  9.86 us
    gather x3, local copies, waits for them, and re-layouts, masked_rows(): taken = source[clipped]  4.94 us
  transfers between devices with their start and end apart: 6, of which 4 were waited for; matrix products, arithmetic and copies ran while one was open for 13% of the time, Pallas kernels for 0%

commit v1 on v0

v1 whole, which is shorter than its diff:
```python
import jax
import jax.numpy as jnp
from jax import lax
from jax.experimental import pallas as pl
from jax.experimental.pallas import tpu as pltpu
from jax.sharding import PartitionSpec as P

MESH = pl.DeviceIdType.MESH
f32, bf16 = jnp.float32, jnp.bfloat16
RHS, LEAF, RANK, LEAVES, NEAR, MIDS = 32, 256, 64, 24, 6, 6
COLS = LEAVES * LEAF
PARTS = 4
ITEMS = 10


def nn(x, w):
    return lax.dot_general(x, w, (((1,), (0,)), ((), ())), preferred_element_type=f32)


def nt(x, w):
    return lax.dot_general(x, w, (((1,), (1,)), ((), ())), preferred_element_type=f32)


def split(value):
    high = value.astype(bf16).astype(f32)
    lane = lax.broadcasted_iota(jnp.int32, value.shape, 1)
    return jnp.where(lane < RANK, high, value - high).astype(bf16)


def halves(w):
    both = jnp.concatenate([w, w], axis=1)
    high = both.astype(bf16)
    return high, (both - high.astype(f32)).astype(bf16)


def twice(x):
    return jnp.concatenate([x, x], axis=1)


def apply_nn(x, pair):
    high, low = pair[:, :128], pair[:, 128:]
    return nn(twice(x), jnp.concatenate([high, high, low, low], axis=0))


def apply_nt(x, pair):
    return nt(twice(x), jnp.concatenate([pair, pair], axis=0))


def place_of(partner, base, empty):
    absent = -jnp.minimum(partner, 0)
    at = (partner - base) * (1 - absent) + empty * absent
    return jnp.minimum(jnp.maximum(at, 0), empty)


def kernel(
    near_list, leaf_parent, mid_pairs, node_pairs, branch_pairs,
    rhs, blocks, basis, upward, mid_coupling, mid_transfer, node_coupling, node_transfer,
    branch_coupling, out,
    rhs_buf, window, block_buf, basis_buf, up_raw, mid_coupling_raw, mid_transfer_raw, node_coupling_raw,
    transfer_raw, branch_coupling_raw, up_pair, mid_transfer_pair, raised, mid_window, mid_field,
    column, gather_a, gather_b, total,
    load_sem, block_sem, halo_send, halo_recv, mid_send, mid_recv, transfer_send, transfer_recv,
    column_send, column_recv, line_send, line_recv, plane_send, plane_recv, out_sem,
):
    b, s = lax.axis_index("branch"), lax.axis_index("sub")
    core, z, x = b % 2, (b // 2) % 4, b // 8
    me = b * 4 + s
    place = core * 4 + s

    def device(at):
        return (at // 4, at % 4)

    right, left = device((me + 1) % 128), device((me + 127) % 128)
    column_peers = []
    for d in range(1, 8):
        at = (place + d) % 8
        column_peers.append((x * 8 + z * 2 + at // 4, at % 4))
    x_peers = [(((x + d) % 4) * 8 + z * 2 + core, s) for d in (1, 2, 3)]
    z_peers = [(x * 8 + ((z + d) % 4) * 2 + core, s) for d in (1, 2, 3)]
    other_core = (x * 8 + z * 2 + 1 - core, s)
    peers = [right, left] + column_peers + x_peers + z_peers

    barrier = pltpu.get_barrier_semaphore()
    for peer in peers:
        pl.semaphore_signal(barrier, inc=1, device_id=peer, device_id_type=MESH)

    def send(src, dst, send_sem, recv_sem, peer):
        copy = pltpu.make_async_remote_copy(
            src_ref=src, dst_ref=dst, send_sem=send_sem, recv_sem=recv_sem,
            device_id=peer, device_id_type=MESH,
        )
        copy.start()
        return copy

    loads = [
        pltpu.make_async_copy(src, dst, load_sem.at[i])
        for i, (src, dst) in enumerate([
            (rhs, rhs_buf),
            (basis, basis_buf),
            (upward, up_raw),
            (mid_transfer, mid_transfer_raw),
            (node_transfer, transfer_raw.at[core]),
            (mid_coupling, mid_coupling_raw),
            (node_coupling.at[s], node_coupling_raw),
            (branch_coupling.at[0], branch_coupling_raw),
        ])
    ]
    per = LEAVES // PARTS
    block_loads = [
        pltpu.make_async_copy(
            blocks.at[pl.ds(i * per, per)], block_buf.at[pl.ds(i * per, per)], block_sem.at[i]
        )
        for i in range(PARTS)
    ]
    for copy in loads + block_loads:
        copy.start()
    window[3 * LEAVES] = jnp.zeros((RHS, LEAF), bf16)
    mid_window[3 * MIDS] = jnp.zeros((RHS, 128), bf16)
    raised[LEAVES] = jnp.zeros((RHS, 128), f32)
    gather_a[16] = jnp.zeros((ITEMS, 16, 128), bf16)
    gather_b[16] = jnp.zeros((ITEMS, 16, 128), bf16)

    def columns_of(leaf):
        return pl.ds(pl.multiple_of(leaf * LEAF, LEAF), LEAF)

    for copy in loads[:3]:
        copy.wait()

    @pl.loop(0, LEAVES // 6)
    def _(step):
        for i in range(6):
            leaf = step * 6 + i
            own = basis_buf[leaf]
            values = rhs_buf[:, columns_of(leaf)]
            window[LEAVES + leaf] = values
            coef = nt(values, jnp.concatenate([own, own], axis=0))
            pair = jnp.concatenate(halves(up_raw[leaf]), axis=1)
            up_pair[leaf] = pair
            raised[leaf] = apply_nn(split(coef), pair)

    parents = [leaf_parent[0, leaf] for leaf in range(LEAVES)]
    ends = [0]
    for q in range(1, MIDS):
        below = 0
        for parent in parents:
            below = below + jnp.minimum(jnp.maximum(q - parent, 0), 1)
        ends.append(below)
    ends.append(LEAVES)
    mids = []
    for q in range(MIDS):
        value = raised[ends[q]]
        for i in range(1, 6):
            leaf = ends[q] + i
            past = jnp.minimum(jnp.maximum(leaf + 1 - ends[q + 1], 0), 1)
            value = value + raised[leaf * (1 - past) + LEAVES * past]
        mids.append(value)
    loads[3].wait()
    node = jnp.zeros((RHS, 128), f32)
    for q in range(MIDS):
        pair = jnp.concatenate(halves(mid_transfer_raw[q]), axis=1)
        mid_transfer_pair[q] = pair
        coef = split(mids[q])
        mid_window[MIDS + q] = coef
        node = node + apply_nn(coef, pair)
    column[place] = split(node)

    pl.semaphore_wait(barrier, len(peers))
    sends = []
    loads[4].wait()
    sends.append(
        send(transfer_raw.at[core], transfer_raw.at[core], transfer_send, transfer_recv, other_core)
    )
    to_column = [
        send(column.at[place], column.at[place], column_send.at[d], column_recv.at[d], peer)
        for d, peer in enumerate(column_peers)
    ]
    own_mids = mid_window.at[pl.ds(MIDS, MIDS)]
    to_mids = [
        send(own_mids, mid_window.at[pl.ds(0, MIDS)], mid_send.at[0], mid_recv.at[0], right),
        send(own_mids, mid_window.at[pl.ds(2 * MIDS, MIDS)], mid_send.at[1], mid_recv.at[1], left),
    ]
    to_halo = []
    for i in range(PARTS):
        j = PARTS - 1 - i
        to_halo.append(
            send(window.at[pl.ds(LEAVES + j * per, per)], window.at[pl.ds(j * per, per)],
                 halo_send.at[0, j], halo_recv.at[0, j], right)
        )
        to_halo.append(
            send(window.at[pl.ds(LEAVES + i * per, per)],
                 window.at[pl.ds(2 * LEAVES + i * per, per)],
                 halo_send.at[1, i], halo_recv.at[1, i], left)
        )

    for part in range(PARTS):
        block_loads[part].wait()

        @pl.loop(0, per // 3)
        def _(step):
            for i in range(3):
                leaf = part * per + step * 3 + i
                total[:, columns_of(leaf)] = nt(
                    rhs_buf[:, columns_of(leaf)], block_buf[leaf, 0]
                )

    for copy in loads[5:]:
        copy.wait()

    sends[0].wait_recv()
    for copy in to_column:
        copy.wait_recv()
    for half in range(2):
        top = jnp.zeros((RHS, 128), f32)
        for sub in range(4):
            pair = jnp.concatenate(halves(transfer_raw[half, sub]), axis=1)
            top = top + apply_nn(column[half * 4 + sub], pair)
        top = split(top)
        gather_a[z * 4 + x, 8 + half] = top[:16]
        gather_b[x * 4 + z, 8 + half] = top[16:]
    for item in range(8):
        value = column[item]
        gather_a[z * 4 + x, item] = value[:16]
        gather_b[x * 4 + z, item] = value[16:]
    to_lines = [
        send(gather_a.at[z * 4 + x], gather_a.at[z * 4 + x], line_send.at[0, d], line_recv.at[0, d], peer)
        for d, peer in enumerate(x_peers)
    ] + [
        send(gather_b.at[x * 4 + z], gather_b.at[x * 4 + z], line_send.at[1, d], line_recv.at[1, d], peer)
        for d, peer in enumerate(z_peers)
    ]

    for copy in to_mids:
        copy.wait_recv()

    @pl.loop(0, MIDS)
    def _(q):
        field = jnp.zeros((RHS, 128), f32)
        for k in range(4):
            at = place_of(mid_pairs[k, q], me * MIDS - MIDS, 3 * MIDS)
            pair = jnp.concatenate(halves(mid_coupling_raw[q, k]), axis=1)
            field = field + apply_nt(mid_window[at], pair)
        mid_field[q] = field

    for copy in to_lines:
        copy.wait_recv()
    to_planes = [
        send(gather_a.at[pl.ds(z * 4, 4)], gather_a.at[pl.ds(z * 4, 4)], plane_send.at[0, d], plane_recv.at[0, d], peer)
        for d, peer in enumerate(z_peers)
    ] + [
        send(gather_b.at[pl.ds(x * 4, 4)], gather_b.at[pl.ds(x * 4, 4)], plane_send.at[1, d], plane_recv.at[1, d], peer)
        for d, peer in enumerate(x_peers)
    ]

    for copy in to_halo:
        copy.wait_recv()

    @pl.loop(0, LEAVES // 4)
    def _(step):
        for i in range(4):
            leaf = step * 4 + i
            value = total[:, columns_of(leaf)]
            for k in range(1, NEAR):
                at = place_of(near_list[k, leaf], me * LEAVES - LEAVES, 3 * LEAVES)
                value = value + nt(window[at], block_buf[leaf, k])
            total[:, columns_of(leaf)] = value

    for copy in to_planes:
        copy.wait_recv()

    def gathered(partner, branch, item):
        at_x, at_z = branch >> 3, (branch >> 1) & 3
        return jnp.concatenate(
            [
                gather_a[place_of(partner, partner - (at_z * 4 + at_x), 16), item],
                gather_b[place_of(partner, partner - (at_x * 4 + at_z), 16), item],
            ],
            axis=0,
        )

    field = jnp.zeros((RHS, 128), f32)
    for k in range(4):
        partner = branch_pairs[0, k]
        branch = jnp.maximum(partner, 0)
        pair = jnp.concatenate(halves(branch_coupling_raw[k]), axis=1)
        field = field + apply_nt(gathered(partner, branch, 8 + (branch & 1)), pair)
    pair = jnp.concatenate(halves(transfer_raw[core, s]), axis=1)
    field = apply_nt(split(field), pair)
    for k in range(8):
        partner = node_pairs[s, k]
        at = jnp.maximum(partner, 0)
        branch = at >> 2
        pair = jnp.concatenate(halves(node_coupling_raw[k]), axis=1)
        field = field + apply_nt(gathered(partner, branch, (branch & 1) * 4 + (at & 3)), pair)
    node_field = split(field)
    for q in range(MIDS):
        mid_window[q] = split(mid_field[q] + apply_nt(node_field, mid_transfer_pair[q]))

    out_copies = []
    for part in range(PARTS):

        @pl.loop(0, per // 3)
        def _(step):
            for i in range(3):
                leaf = part * per + step * 3 + i
                field = split(apply_nt(mid_window[leaf_parent[0, leaf]], up_pair[leaf]))
                own = basis_buf[leaf]
                far = nn(field, jnp.concatenate([own, own], axis=0))
                total[:, columns_of(leaf)] += far

        at = pl.ds(part * per * LEAF, per * LEAF)
        copy = pltpu.make_async_copy(total.at[:, at], out.at[:, at], out_sem.at[part])
        copy.start()
        out_copies.append(copy)
    for copy in out_copies:
        copy.wait()
    for copy in sends + to_column + to_mids + to_halo + to_lines + to_planes:
        copy.wait_send()


def on_device(
    right_sides, near_blocks, near_list, leaf_basis, leaf_parent, leaf_upward_matrix, mid_pairs,
    mid_coupling, mid_transfer, node_pairs, node_coupling, node_transfer, branch_pairs,
    branch_coupling,
):
    dma = pltpu.SemaphoreType.DMA
    smem = pl.BlockSpec(memory_space=pltpu.SMEM)
    hbm = pl.BlockSpec(memory_space=pltpu.HBM)
    return pl.pallas_call(
        kernel,
        out_shape=jax.ShapeDtypeStruct((RHS, COLS), f32),
        in_specs=[smem] * 5 + [hbm] * 9,
        out_specs=hbm,
        scratch_shapes=[
            pltpu.VMEM((RHS, COLS), bf16),
            pltpu.VMEM((3 * LEAVES + 1, RHS, LEAF), bf16),
            pltpu.VMEM((LEAVES, NEAR, LEAF, LEAF), bf16),
            pltpu.VMEM((LEAVES, RANK, LEAF), bf16),
            pltpu.VMEM((LEAVES, RANK, RANK), f32),
            pltpu.VMEM((MIDS, 4, RANK, RANK), f32),
            pltpu.VMEM((MIDS, RANK, RANK), f32),
            pltpu.VMEM((8, RANK, RANK), f32),
            pltpu.VMEM((2, 4, RANK, RANK), f32),
            pltpu.VMEM((4, RANK, RANK), f32),
            pltpu.VMEM((LEAVES, RANK, 256), bf16),
            pltpu.VMEM((MIDS, RANK, 256), bf16),
            pltpu.VMEM((LEAVES + 1, RHS, 128), f32),
            pltpu.VMEM((3 * MIDS + 1, RHS, 128), bf16),
            pltpu.VMEM((MIDS, RHS, 128), f32),
            pltpu.VMEM((8, RHS, 128), bf16),
            pltpu.VMEM((17, ITEMS, 16, 128), bf16),
            pltpu.VMEM((17, ITEMS, 16, 128), bf16),
            pltpu.VMEM((RHS, COLS), f32),
            dma((8,)), dma((PARTS,)), dma((2, PARTS)), dma((2, PARTS)), dma((2,)), dma((2,)),
            dma, dma, dma((7,)), dma((7,)), dma((2, 3)), dma((2, 3)), dma((2, 3)), dma((2, 3)),
            dma((PARTS,)),
        ],
        compiler_params=pltpu.CompilerParams(
            collective_id=0, has_side_effects=True, vmem_limit_bytes=62 * 2**20
        ),
        cost_estimate=pl.CostEstimate(
            flops=10**9, bytes_accessed=24 * 10**6, transcendentals=0
        ),
    )(
        near_list.T, leaf_parent, mid_pairs.T, node_pairs, branch_pairs,
        right_sides, near_blocks, leaf_basis, leaf_upward_matrix, mid_coupling, mid_transfer,
        node_coupling, node_transfer, branch_coupling,
    )


def solution(mesh):
    rows = ("branch", "sub")
    return jax.shard_map(
        on_device,
        mesh=mesh,
        in_specs=(
            P(None, rows),
            P(rows, None, None, None),
            P(rows, None),
            P(rows, None, None),
            P(rows, None),
            P(rows, None, None),
            P(rows, None),
            P(rows, None, None, None),
            P(rows, None, None),
            P("branch", None),
            P("branch", None, None, None),
            P("branch", None, None),
            P("branch", None),
            P("branch", None, None, None),
        ),
        out_specs=P(None, rows),
        check_vma=False,
    )
```

time: 168 us -> 42.5 us (0.25)
  waiting for transfers between devices: 101 us -> 0 us
  Pallas kernels: 0 us -> 39.9 us
  matrix products: 25.4 us -> 0 us
  between operations: 13.7 us -> 0.01 us
  starting transfers between devices: 12.5 us -> 0 us
  local copies, waits for them, and re-layouts: 9.93 us -> 2.06 us
  other arithmetic: 4.57 us -> 0 us
    all_gather x2 -> x0, waiting for transfers between devices: 98.2 us -> none  [the longest x1 63.5 us: on_device(): lax.all_gather(top_term[None], ('branch', 'sub'), axis=0, tiled=True)]
    pallas_call x0 -> x1, Pallas kernels: none -> 39.9 us  [on_device(): pl.pallas_call(kernel, out_shape=jax.ShapeDtypeStruct((RHS, COLS), f32),...]
    dot_general x14 -> x0, matrix products: 25.4 us -> none  [the longest x1 10.3 us: on_device(): jnp.einsum('ikab,nikb->nia', near_blocks, picked, preferred_element_type=...]
    ppermute x4 -> x0, starting transfers between devices: 12.4 us -> none  [the longest x2 9.86 us: with_halo(): lax.ppermute(tail, axis, [(i, (i + 1) % count) for i in range(ends)])]
    gather x4 -> x0, local copies, waits for them, and re-layouts: 7 us -> none  [the longest x3 4.94 us: masked_rows(): taken = source[clipped]]
    reduce_sum x1 -> x0, other arithmetic: 2.8 us -> none  [on_device(): all_terms.reshape(branches, sub_count, rhs_count, basis_rank).sum(axis=1)]
    ppermute x4 -> x0, waiting for transfers between devices: 2.36 us -> none  [the longest x2 2.3 us: with_halo(): lax.ppermute(tail, axis, [(i, (i + 1) % count) for i in range(ends)])]
    unnamed x24 -> x1, local copies, waits for them, and re-layouts: 0.05 us -> 2.06 us
  transfers between devices with their start and end apart: 6 -> 0, of which waited for: 4 -> 0; matrix products, arithmetic and copies ran while one was open for 13% -> 0% of each run, Pallas kernels for 0% -> 0%
where the time goes in v1:
time: 42.5 us; the launch traced here: 41.9 us
  Pallas kernels  39.9 us (94%)
  local copies, waits for them, and re-layouts  2.06 us (5%)
    pallas_call x1, Pallas kernels, on_device(): pl.pallas_call(kernel, out_shape=jax.ShapeDtypeStruct((RHS, COLS), f32),...  39.9 us
    unnamed x1, local copies, waits for them, and re-layouts  2.06 us

profile of v1, /device:TPU:0, one launch (start us, length us, event | category | flops | bytes accessed | tf_op | source)
XLA Modules:
  0.0 41.9 jit_solution(13147612732898332566)
XLA Ops:
  0.0 39.9 %shard_map.136 = f32[32,6144]{1,0:T(8,128)} custom-call(s32[6,24]{1,0:T(8,128)} %bitcast.2, s32[1,24]{1,0:T(1,128)} %leaf_parent.1, s32[4,6]{1,0:T(4,128)} %bitcast.3, s32[4,8]{1,0:T(4,128)} %node_pairs.1, s32[1,4]{1,0:T(1,128)} %branch_pairs.1, bf16[32,6144]{1,0:T(8,128)(2,1)} %rhs.1, bf16[24,6,256,256]{3,2,1,0:T(8,128)(2,1)} %blocks.1, ...), custom_call_target="tpu_custom_call" | custom-call | flops 1000000000 | bytes 24000000 | tf_op jit(solution)/shard_map/pallas_call | solution.py:328
  39.9 2.1 %copy.16 = f32[32,6144]{1,0:T(8,128)} copy(f32[32,6144]{1,0:T(8,128)} %shard_map.136) | data formatting | bytes 1572864

commit v2 on v1

--- a/solution.py
+++ b/solution.py
@@ -10,6 +10,9 @@
 RHS, LEAF, RANK, LEAVES, NEAR, MIDS = 32, 256, 64, 24, 6, 6
 COLS = LEAVES * LEAF
 PARTS = 4
+GROUP = 8
+EARLY = 1
+SLOTS = 12
 ITEMS = 10
 
 
@@ -33,6 +36,10 @@
     return high, (both - high.astype(f32)).astype(bf16)
 
 
+def pair_of(w):
+    return jnp.concatenate(halves(w), axis=1)
+
+
 def twice(x):
     return jnp.concatenate([x, x], axis=1)
 
@@ -56,11 +63,13 @@
     near_list, leaf_parent, mid_pairs, node_pairs, branch_pairs,
     rhs, blocks, basis, upward, mid_coupling, mid_transfer, node_coupling, node_transfer,
     branch_coupling, out,
-    rhs_buf, window, block_buf, basis_buf, up_raw, mid_coupling_raw, mid_transfer_raw, node_coupling_raw,
-    transfer_raw, branch_coupling_raw, up_pair, mid_transfer_pair, raised, mid_window, mid_field,
-    column, gather_a, gather_b, total,
+    rhs_buf, window, block_buf, basis_buf, up_raw, mid_coupling_raw, mid_transfer_raw,
+    node_coupling_raw, transfer_raw, branch_coupling_raw, up_pair, mid_transfer_pair,
+    transfer_pair, coupling_pair, raised, mid_window, mid_field, column, line_a, line_b, chosen_a,
+    chosen_b, got_a, got_b, total, peer_nodes, peer_branches, choice,
     load_sem, block_sem, halo_send, halo_recv, mid_send, mid_recv, transfer_send, transfer_recv,
-    column_send, column_recv, line_send, line_recv, plane_send, plane_recv, out_sem,
+    column_send, column_recv, pair_send, pair_recv, line_send, line_recv, plane_send, plane_recv,
+    out_sem,
 ):
     b, s = lax.axis_index("branch"), lax.axis_index("sub")
     core, z, x = b % 2, (b // 2) % 4, b // 8
@@ -117,8 +126,8 @@
     window[3 * LEAVES] = jnp.zeros((RHS, LEAF), bf16)
     mid_window[3 * MIDS] = jnp.zeros((RHS, 128), bf16)
     raised[LEAVES] = jnp.zeros((RHS, 128), f32)
-    gather_a[16] = jnp.zeros((ITEMS, 16, 128), bf16)
-    gather_b[16] = jnp.zeros((ITEMS, 16, 128), bf16)
+    got_a[4 * SLOTS] = jnp.zeros((16, 128), bf16)
+    got_b[4 * SLOTS] = jnp.zeros((16, 128), bf16)
 
     def columns_of(leaf):
         return pl.ds(pl.multiple_of(leaf * LEAF, LEAF), LEAF)
@@ -126,17 +135,17 @@
     for copy in loads[:3]:
         copy.wait()
 
-    @pl.loop(0, LEAVES // 6)
-    def _(step):
-        for i in range(6):
-            leaf = step * 6 + i
+    for first in range(0, LEAVES, GROUP):
+        group = range(first, first + GROUP)
+        coefs = []
+        for leaf in group:
+            values = rhs_buf[:, leaf * LEAF : (leaf + 1) * LEAF]
+            window[LEAVES + leaf] = values
             own = basis_buf[leaf]
-            values = rhs_buf[:, columns_of(leaf)]
-            window[LEAVES + leaf] = values
-            coef = nt(values, jnp.concatenate([own, own], axis=0))
-            pair = jnp.concatenate(halves(up_raw[leaf]), axis=1)
-            up_pair[leaf] = pair
-            raised[leaf] = apply_nn(split(coef), pair)
+            coefs.append(nt(values, jnp.concatenate([own, own], axis=0)))
+            up_pair[leaf] = pair_of(up_raw[leaf])
+        for leaf, coef in zip(group, coefs):
+            raised[leaf] = apply_nn(split(coef), up_pair[leaf])
 
     parents = [leaf_parent[0, leaf] for leaf in range(LEAVES)]
     ends = [0]
@@ -165,91 +174,140 @@
     column[place] = split(node)
 
     pl.semaphore_wait(barrier, len(peers))
-    sends = []
-    loads[4].wait()
-    sends.append(
-        send(transfer_raw.at[core], transfer_raw.at[core], transfer_send, transfer_recv, other_core)
-    )
     to_column = [
         send(column.at[place], column.at[place], column_send.at[d], column_recv.at[d], peer)
         for d, peer in enumerate(column_peers)
+    ]
+    loads[4].wait()
+    to_core = send(
+        transfer_raw.at[core], transfer_raw.at[core], transfer_send, transfer_recv, other_core
+    )
+    to_choose = []
+    for d, peer in enumerate(z_peers + x_peers):
+        to_choose.append(
+            send(node_pairs, peer_nodes.at[d], pair_send.at[0, d], pair_recv.at[0, d], peer)
+        )
+        to_choose.append(
+            send(branch_pairs, peer_branches.at[d], pair_send.at[1, d], pair_recv.at[1, d], peer)
+        )
+
+    def halo(i):
+        j = PARTS - 1 - i
+        return [
+            send(window.at[pl.ds(LEAVES + j * per, per)], window.at[pl.ds(j * per, per)],
+                 halo_send.at[0, j], halo_recv.at[0, j], right),
+            send(window.at[pl.ds(LEAVES + i * per, per)],
+                 window.at[pl.ds(2 * LEAVES + i * per, per)],
+                 halo_send.at[1, i], halo_recv.at[1, i], left),
+        ]
+
+    to_halo = []
+    for i in range(EARLY):
+        to_halo += halo(i)
+
+    def near_self(part):
+        block_loads[part].wait()
+        for leaf in range(part * per, part * per + per):
+            total[:, leaf * LEAF : (leaf + 1) * LEAF] = nt(
+                rhs_buf[:, leaf * LEAF : (leaf + 1) * LEAF], block_buf[leaf, 0]
+            )
+
+    for sub in range(4):
+        transfer_pair[core * 4 + sub] = pair_of(transfer_raw[core, sub])
+    for part in range(PARTS // 2):
+        near_self(part)
+
+    to_core.wait_recv()
+    for sub in range(4):
+        transfer_pair[(1 - core) * 4 + sub] = pair_of(transfer_raw[1 - core, sub])
+    for copy in to_column:
+        copy.wait_recv()
+    for half in range(2):
+        top = jnp.zeros((RHS, 128), f32)
+        for sub in range(4):
+            item = half * 4 + sub
+            top = top + apply_nn(column[item], transfer_pair[item])
+        top = split(top)
+        line_a[x * ITEMS + 8 + half] = top[:16]
+        line_b[z * ITEMS + 8 + half] = top[16:]
+    for item in range(8):
+        value = column[item]
+        line_a[x * ITEMS + item] = value[:16]
+        line_b[z * ITEMS + item] = value[16:]
+    own_a, own_b = line_a.at[pl.ds(x * ITEMS, ITEMS)], line_b.at[pl.ds(z * ITEMS, ITEMS)]
+    to_lines = [
+        send(own_a, own_a, line_send.at[0, d], line_recv.at[0, d], peer)
+        for d, peer in enumerate(x_peers)
+    ] + [
+        send(own_b, own_b, line_send.at[1, d], line_recv.at[1, d], peer)
+        for d, peer in enumerate(z_peers)
     ]
     own_mids = mid_window.at[pl.ds(MIDS, MIDS)]
     to_mids = [
         send(own_mids, mid_window.at[pl.ds(0, MIDS)], mid_send.at[0], mid_recv.at[0], right),
         send(own_mids, mid_window.at[pl.ds(2 * MIDS, MIDS)], mid_send.at[1], mid_recv.at[1], left),
     ]
-    to_halo = []
-    for i in range(PARTS):
-        j = PARTS - 1 - i
-        to_halo.append(
-            send(window.at[pl.ds(LEAVES + j * per, per)], window.at[pl.ds(j * per, per)],
-                 halo_send.at[0, j], halo_recv.at[0, j], right)
-        )
-        to_halo.append(
-            send(window.at[pl.ds(LEAVES + i * per, per)],
-                 window.at[pl.ds(2 * LEAVES + i * per, per)],
-                 halo_send.at[1, i], halo_recv.at[1, i], left)
-        )
-
-    for part in range(PARTS):
-        block_loads[part].wait()
-
-        @pl.loop(0, per // 3)
-        def _(step):
-            for i in range(3):
-                leaf = part * per + step * 3 + i
-                total[:, columns_of(leaf)] = nt(
-                    rhs_buf[:, columns_of(leaf)], block_buf[leaf, 0]
-                )
-
+    for i in range(EARLY, PARTS):
+        to_halo += halo(i)
+
+    def spot(node, item):
+        branch = node if item else node >> 2
+        inside = 8 + (branch & 1) if item else (branch & 1) * 4 + (node & 3)
+        return branch >> 3, (branch >> 1) & 3, inside
+
+    for copy in to_choose:
+        copy.wait_recv()
+    for d in range(6):
+        for k in range(SLOTS):
+            if k < 4:
+                at = spot(jnp.maximum(peer_branches[d, 0, k], 0), True)
+            else:
+                at = spot(jnp.maximum(peer_nodes[d, s, k - 4], 0), False)
+            choice[d * SLOTS + k] = at[0 if d < 3 else 1] * ITEMS + at[2]
+    own_choice, absent = [], []
+    for k in range(SLOTS):
+        partner = branch_pairs[0, k] if k < 4 else node_pairs[s, k - 4]
+        own_choice.append(spot(jnp.maximum(partner, 0), k < 4))
+        absent.append(partner)
+
+    for part in range(PARTS // 2, PARTS):
+        near_self(part)
     for copy in loads[5:]:
         copy.wait()
-
-    sends[0].wait_recv()
-    for copy in to_column:
-        copy.wait_recv()
-    for half in range(2):
-        top = jnp.zeros((RHS, 128), f32)
-        for sub in range(4):
-            pair = jnp.concatenate(halves(transfer_raw[half, sub]), axis=1)
-            top = top + apply_nn(column[half * 4 + sub], pair)
-        top = split(top)
-        gather_a[z * 4 + x, 8 + half] = top[:16]
-        gather_b[x * 4 + z, 8 + half] = top[16:]
-    for item in range(8):
-        value = column[item]
-        gather_a[z * 4 + x, item] = value[:16]
-        gather_b[x * 4 + z, item] = value[16:]
-    to_lines = [
-        send(gather_a.at[z * 4 + x], gather_a.at[z * 4 + x], line_send.at[0, d], line_recv.at[0, d], peer)
-        for d, peer in enumerate(x_peers)
-    ] + [
-        send(gather_b.at[x * 4 + z], gather_b.at[x * 4 + z], line_send.at[1, d], line_recv.at[1, d], peer)
-        for d, peer in enumerate(z_peers)
-    ]
+    for k in range(4):
+        coupling_pair[k] = pair_of(branch_coupling_raw[k])
+    for k in range(8):
+        coupling_pair[4 + k] = pair_of(node_coupling_raw[k])
+
+    for copy in to_lines:
+        copy.wait_recv()
+    to_planes = []
+    for d in range(3):
+        for k in range(SLOTS):
+            chosen_a[d * SLOTS + k] = line_a[choice[(2 - d) * SLOTS + k]]
+            chosen_b[d * SLOTS + k] = line_b[choice[(5 - d) * SLOTS + k]]
+        at = pl.ds(d * SLOTS, SLOTS)
+        to_planes.append(
+            send(chosen_a.at[at], got_a.at[pl.ds(z * SLOTS, SLOTS)],
+                 plane_send.at[0, d], plane_recv.at[0, d], z_peers[d])
+        )
+        to_planes.append(
+            send(chosen_b.at[at], got_b.at[pl.ds(x * SLOTS, SLOTS)],
+                 plane_send.at[1, d], plane_recv.at[1, d], x_peers[d])
+        )
+    for k in range(SLOTS):
+        at_x, at_z, item = own_choice[k]
+        got_a[z * SLOTS + k] = line_a[at_x * ITEMS + item]
+        got_b[x * SLOTS + k] = line_b[at_z * ITEMS + item]
 
     for copy in to_mids:
         copy.wait_recv()
-
-    @pl.loop(0, MIDS)
-    def _(q):
+    for q in range(MIDS):
         field = jnp.zeros((RHS, 128), f32)
         for k in range(4):
             at = place_of(mid_pairs[k, q], me * MIDS - MIDS, 3 * MIDS)
-            pair = jnp.concatenate(halves(mid_coupling_raw[q, k]), axis=1)
-            field = field + apply_nt(mid_window[at], pair)
+            field = field + apply_nt(mid_window[at], pair_of(mid_coupling_raw[q, k]))
         mid_field[q] = field
-
-    for copy in to_lines:
-        copy.wait_recv()
-    to_planes = [
-        send(gather_a.at[pl.ds(z * 4, 4)], gather_a.at[pl.ds(z * 4, 4)], plane_send.at[0, d], plane_recv.at[0, d], peer)
-        for d, peer in enumerate(z_peers)
-    ] + [
-        send(gather_b.at[pl.ds(x * 4, 4)], gather_b.at[pl.ds(x * 4, 4)], plane_send.at[1, d], plane_recv.at[1, d], peer)
-        for d, peer in enumerate(x_peers)
-    ]
 
     for copy in to_halo:
         copy.wait_recv()
@@ -267,53 +325,42 @@
     for copy in to_planes:
         copy.wait_recv()
 
-    def gathered(partner, branch, item):
-        at_x, at_z = branch >> 3, (branch >> 1) & 3
+    def gathered(k):
+        at_x, at_z, _ = own_choice[k]
         return jnp.concatenate(
             [
-                gather_a[place_of(partner, partner - (at_z * 4 + at_x), 16), item],
-                gather_b[place_of(partner, partner - (at_x * 4 + at_z), 16), item],
+                got_a[place_of(absent[k], absent[k] - (at_z * SLOTS + k), 4 * SLOTS)],
+                got_b[place_of(absent[k], absent[k] - (at_x * SLOTS + k), 4 * SLOTS)],
             ],
             axis=0,
         )
 
     field = jnp.zeros((RHS, 128), f32)
     for k in range(4):
-        partner = branch_pairs[0, k]
-        branch = jnp.maximum(partner, 0)
-        pair = jnp.concatenate(halves(branch_coupling_raw[k]), axis=1)
-        field = field + apply_nt(gathered(partner, branch, 8 + (branch & 1)), pair)
-    pair = jnp.concatenate(halves(transfer_raw[core, s]), axis=1)
-    field = apply_nt(split(field), pair)
-    for k in range(8):
-        partner = node_pairs[s, k]
-        at = jnp.maximum(partner, 0)
-        branch = at >> 2
-        pair = jnp.concatenate(halves(node_coupling_raw[k]), axis=1)
-        field = field + apply_nt(gathered(partner, branch, (branch & 1) * 4 + (at & 3)), pair)
+        field = field + apply_nt(gathered(k), coupling_pair[k])
+    nodes_field = jnp.zeros((RHS, 128), f32)
+    for k in range(4, SLOTS):
+        nodes_field = nodes_field + apply_nt(gathered(k), coupling_pair[k])
+    field = nodes_field + apply_nt(split(field), transfer_pair[place])
     node_field = split(field)
     for q in range(MIDS):
         mid_window[q] = split(mid_field[q] + apply_nt(node_field, mid_transfer_pair[q]))
 
     out_copies = []
     for part in range(PARTS):
-
-        @pl.loop(0, per // 3)
-        def _(step):
-            for i in range(3):
-                leaf = part * per + step * 3 + i
-                field = split(apply_nt(mid_window[leaf_parent[0, leaf]], up_pair[leaf]))
-                own = basis_buf[leaf]
-                far = nn(field, jnp.concatenate([own, own], axis=0))
-                total[:, columns_of(leaf)] += far
-
+        group = range(part * per, part * per + per)
+        fields = [split(apply_nt(mid_window[leaf_parent[0, leaf]], up_pair[leaf])) for leaf in group]
+        for leaf, field in zip(group, fields):
+            own = basis_buf[leaf]
+            far = nn(field, jnp.concatenate([own, own], axis=0))
+            total[:, leaf * LEAF : (leaf + 1) * LEAF] += far
         at = pl.ds(part * per * LEAF, per * LEAF)
         copy = pltpu.make_async_copy(total.at[:, at], out.at[:, at], out_sem.at[part])
         copy.start()
         out_copies.append(copy)
     for copy in out_copies:
         copy.wait()
-    for copy in sends + to_column + to_mids + to_halo + to_lines + to_planes:
+    for copy in [to_core] + to_column + to_choose + to_mids + to_halo + to_lines + to_planes:
         copy.wait_send()
 
 
@@ -343,15 +390,24 @@
             pltpu.VMEM((4, RANK, RANK), f32),
             pltpu.VMEM((LEAVES, RANK, 256), bf16),
             pltpu.VMEM((MIDS, RANK, 256), bf16),
+            pltpu.VMEM((8, RANK, 256), bf16),
+            pltpu.VMEM((SLOTS, RANK, 256), bf16),
             pltpu.VMEM((LEAVES + 1, RHS, 128), f32),
             pltpu.VMEM((3 * MIDS + 1, RHS, 128), bf16),
             pltpu.VMEM((MIDS, RHS, 128), f32),
             pltpu.VMEM((8, RHS, 128), bf16),
-            pltpu.VMEM((17, ITEMS, 16, 128), bf16),
-            pltpu.VMEM((17, ITEMS, 16, 128), bf16),
+            pltpu.VMEM((4 * ITEMS, 16, 128), bf16),
+            pltpu.VMEM((4 * ITEMS, 16, 128), bf16),
+            pltpu.VMEM((3 * SLOTS, 16, 128), bf16),
+            pltpu.VMEM((3 * SLOTS, 16, 128), bf16),
+            pltpu.VMEM((4 * SLOTS + 1, 16, 128), bf16),
+            pltpu.VMEM((4 * SLOTS + 1, 16, 128), bf16),
             pltpu.VMEM((RHS, COLS), f32),
+            pltpu.SMEM((6, 4, 8), jnp.int32),
+            pltpu.SMEM((6, 1, 4), jnp.int32),
+            pltpu.SMEM((6 * SLOTS,), jnp.int32),
             dma((8,)), dma((PARTS,)), dma((2, PARTS)), dma((2, PARTS)), dma((2,)), dma((2,)),
-            dma, dma, dma((7,)), dma((7,)), dma((2, 3)), dma((2, 3)), dma((2, 3)), dma((2, 3)),
+            dma, dma, dma((7,)), dma((7,)), dma((2, 6)), dma((2, 6)), dma((2, 3)), dma((2, 3)), dma((2, 3)), dma((2, 3)),
             dma((PARTS,)),
         ],
         compiler_params=pltpu.CompilerParams(

time: 42.5 us -> 34.8 us (0.82)
  Pallas kernels: 39.9 us -> 32.5 us
    pallas_call x1, Pallas kernels: 39.9 us -> 32.5 us  [on_device(): pl.pallas_call(kernel, out_shape=jax.ShapeDtypeStruct((RHS, COLS), f32),...]
where the time goes in v2:
time: 34.8 us; the launch traced here: 34.6 us
  Pallas kernels  32.5 us (93%)
  local copies, waits for them, and re-layouts  2.06 us (6%)
    pallas_call x1, Pallas kernels, on_device(): pl.pallas_call(kernel, out_shape=jax.ShapeDtypeStruct((RHS, COLS), f32),...  32.5 us
    unnamed x1, local copies, waits for them, and re-layouts  2.06 us

profile of v2, /device:TPU:0, one launch (start us, length us, event | category | flops | bytes accessed | tf_op | source)
XLA Modules:
  0.0 34.6 jit_solution(3911981897261193787)
XLA Ops:
  0.0 32.5 %shard_map.136 = f32[32,6144]{1,0:T(8,128)} custom-call(s32[6,24]{1,0:T(8,128)} %bitcast.2, s32[1,24]{1,0:T(1,128)} %leaf_parent.1, s32[4,6]{1,0:T(4,128)} %bitcast.3, s32[4,8]{1,0:T(4,128)} %node_pairs.1, s32[1,4]{1,0:T(1,128)} %branch_pairs.1, bf16[32,6144]{1,0:T(8,128)(2,1)} %rhs.1, bf16[24,6,256,256]{3,2,1,0:T(8,128)(2,1)} %blocks.1, ...), custom_call_target="tpu_custom_call" | custom-call | flops 1000000000 | bytes 24000000 | tf_op jit(solution)/shard_map/pallas_call | solution.py:375
  32.5 2.1 %copy.16 = f32[32,6144]{1,0:T(8,128)} copy(f32[32,6144]{1,0:T(8,128)} %shard_map.136) | data formatting | bytes 1572864

commit v3 on v2

--- a/solution.py
+++ b/solution.py
@@ -11,7 +11,11 @@
 COLS = LEAVES * LEAF
 PARTS = 4
 GROUP = 8
-EARLY = 1
+THIRD = 3
+STAGES = 4
+FIRST = LEAVES - (STAGES - 1) * THIRD
+SECOND = 12
+BESIDE_LINE = 1
 SLOTS = 12
 ITEMS = 10
 
@@ -63,7 +67,7 @@
     near_list, leaf_parent, mid_pairs, node_pairs, branch_pairs,
     rhs, blocks, basis, upward, mid_coupling, mid_transfer, node_coupling, node_transfer,
     branch_coupling, out,
-    rhs_buf, window, block_buf, basis_buf, up_raw, mid_coupling_raw, mid_transfer_raw,
+    rhs_buf, window, late, block_buf, basis_buf, up_raw, mid_coupling_raw, mid_transfer_raw,
     node_coupling_raw, transfer_raw, branch_coupling_raw, up_pair, mid_transfer_pair,
     transfer_pair, coupling_pair, raised, mid_window, mid_field, column, line_a, line_b, chosen_a,
     chosen_b, got_a, got_b, total, peer_nodes, peer_branches, choice,
@@ -121,9 +125,10 @@
         )
         for i in range(PARTS)
     ]
-    for copy in loads + block_loads:
+    for copy in loads[:3]:
         copy.start()
-    window[3 * LEAVES] = jnp.zeros((RHS, LEAF), bf16)
+    for leaf in [*range(LEAVES - FIRST), *range(2 * LEAVES + FIRST, 3 * LEAVES + 1)]:
+        window[leaf] = jnp.zeros((RHS, LEAF), bf16)
     mid_window[3 * MIDS] = jnp.zeros((RHS, 128), bf16)
     raised[LEAVES] = jnp.zeros((RHS, 128), f32)
     got_a[4 * SLOTS] = jnp.zeros((16, 128), bf16)
@@ -134,18 +139,40 @@
 
     for copy in loads[:3]:
         copy.wait()
+    for copy in loads[3:] + block_loads:
+        copy.start()
+    for leaf in range(LEAVES):
+        window[LEAVES + leaf] = rhs_buf[:, leaf * LEAF : (leaf + 1) * LEAF]
+    def send_halo(stage):
+        if stage < 0:
+            size = -stage
+            begin = FIRST - size if stage == -SECOND else 0
+            end = begin + size
+            there = [window.at[pl.ds(LEAVES - end, size)], window.at[pl.ds(2 * LEAVES + begin, size)]]
+        else:
+            size, end = THIRD, FIRST + (stage + 1) * THIRD
+            there = [late.at[stage, 0], late.at[stage, 1]]
+        here = [window.at[pl.ds(2 * LEAVES - end, size)], window.at[pl.ds(LEAVES + end - size, size)]]
+        slot = stage + 2 if stage >= 0 else (1 if stage == -SECOND else 0)
+        return [
+            send(here[i], there[i], halo_send.at[i, slot], halo_recv.at[i, slot], peer)
+            for i, peer in enumerate((right, left))
+        ]
+
 
     for first in range(0, LEAVES, GROUP):
         group = range(first, first + GROUP)
         coefs = []
         for leaf in group:
             values = rhs_buf[:, leaf * LEAF : (leaf + 1) * LEAF]
-            window[LEAVES + leaf] = values
             own = basis_buf[leaf]
             coefs.append(nt(values, jnp.concatenate([own, own], axis=0)))
             up_pair[leaf] = pair_of(up_raw[leaf])
         for leaf, coef in zip(group, coefs):
             raised[leaf] = apply_nn(split(coef), up_pair[leaf])
+
+    pl.semaphore_wait(barrier, len(peers))
+    to_halo = send_halo(SECOND - FIRST)
 
     parents = [leaf_parent[0, leaf] for leaf in range(LEAVES)]
     ends = [0]
@@ -173,7 +200,6 @@
         node = node + apply_nn(coef, pair)
     column[place] = split(node)
 
-    pl.semaphore_wait(barrier, len(peers))
     to_column = [
         send(column.at[place], column.at[place], column_send.at[d], column_recv.at[d], peer)
         for d, peer in enumerate(column_peers)
@@ -191,19 +217,14 @@
             send(branch_pairs, peer_branches.at[d], pair_send.at[1, d], pair_recv.at[1, d], peer)
         )
 
-    def halo(i):
-        j = PARTS - 1 - i
-        return [
-            send(window.at[pl.ds(LEAVES + j * per, per)], window.at[pl.ds(j * per, per)],
-                 halo_send.at[0, j], halo_recv.at[0, j], right),
-            send(window.at[pl.ds(LEAVES + i * per, per)],
-                 window.at[pl.ds(2 * LEAVES + i * per, per)],
-                 halo_send.at[1, i], halo_recv.at[1, i], left),
-        ]
-
-    to_halo = []
-    for i in range(EARLY):
-        to_halo += halo(i)
+    own_mids = mid_window.at[pl.ds(MIDS, MIDS)]
+    to_mids = [
+        send(own_mids, mid_window.at[pl.ds(0, MIDS)], mid_send.at[0], mid_recv.at[0], right),
+        send(own_mids, mid_window.at[pl.ds(2 * MIDS, MIDS)], mid_send.at[1], mid_recv.at[1], left),
+    ]
+    to_halo += send_halo(-SECOND)
+    for stage in range(STAGES - 1):
+        to_halo += send_halo(stage)
 
     def near_self(part):
         block_loads[part].wait()
@@ -242,13 +263,24 @@
         send(own_b, own_b, line_send.at[1, d], line_recv.at[1, d], peer)
         for d, peer in enumerate(z_peers)
     ]
-    own_mids = mid_window.at[pl.ds(MIDS, MIDS)]
-    to_mids = [
-        send(own_mids, mid_window.at[pl.ds(0, MIDS)], mid_send.at[0], mid_recv.at[0], right),
-        send(own_mids, mid_window.at[pl.ds(2 * MIDS, MIDS)], mid_send.at[1], mid_recv.at[1], left),
-    ]
-    for i in range(EARLY, PARTS):
-        to_halo += halo(i)
+
+    def near_others(stage):
+        for copy in to_halo[2 * stage + 2 : 2 * stage + 4] if stage else to_halo[:4]:
+            copy.wait_recv()
+        end = FIRST + stage * THIRD
+        if stage:
+            for i in range(THIRD):
+                window[LEAVES - end + i] = late[stage - 1, 0, i]
+                window[2 * LEAVES + end - THIRD + i] = late[stage - 1, 1, i]
+            leaves = [*range(LEAVES - end, LEAVES - end + THIRD), *range(end - THIRD, end)]
+        else:
+            leaves = range(LEAVES - end, end)
+        for leaf in leaves:
+            value = total[:, leaf * LEAF : (leaf + 1) * LEAF]
+            for k in range(1, NEAR):
+                at = place_of(near_list[k, leaf], me * LEAVES - LEAVES, 3 * LEAVES)
+                value = value + nt(window[at], block_buf[leaf, k])
+            total[:, leaf * LEAF : (leaf + 1) * LEAF] = value
 
     def spot(node, item):
         branch = node if item else node >> 2
@@ -279,6 +311,9 @@
     for k in range(8):
         coupling_pair[4 + k] = pair_of(node_coupling_raw[k])
 
+    for stage in range(BESIDE_LINE):
+        near_others(stage)
+
     for copy in to_lines:
         copy.wait_recv()
     to_planes = []
@@ -309,18 +344,8 @@
             field = field + apply_nt(mid_window[at], pair_of(mid_coupling_raw[q, k]))
         mid_field[q] = field
 
-    for copy in to_halo:
-        copy.wait_recv()
-
-    @pl.loop(0, LEAVES // 4)
-    def _(step):
-        for i in range(4):
-            leaf = step * 4 + i
-            value = total[:, columns_of(leaf)]
-            for k in range(1, NEAR):
-                at = place_of(near_list[k, leaf], me * LEAVES - LEAVES, 3 * LEAVES)
-                value = value + nt(window[at], block_buf[leaf, k])
-            total[:, columns_of(leaf)] = value
+    for stage in range(BESIDE_LINE, STAGES):
+        near_others(stage)
 
     for copy in to_planes:
         copy.wait_recv()
@@ -380,6 +405,7 @@
         scratch_shapes=[
             pltpu.VMEM((RHS, COLS), bf16),
             pltpu.VMEM((3 * LEAVES + 1, RHS, LEAF), bf16),
+            pltpu.VMEM((STAGES - 1, 2, THIRD, RHS, LEAF), bf16),
             pltpu.VMEM((LEAVES, NEAR, LEAF, LEAF), bf16),
             pltpu.VMEM((LEAVES, RANK, LEAF), bf16),
             pltpu.VMEM((LEAVES, RANK, RANK), f32),
@@ -406,7 +432,7 @@
             pltpu.SMEM((6, 4, 8), jnp.int32),
             pltpu.SMEM((6, 1, 4), jnp.int32),
             pltpu.SMEM((6 * SLOTS,), jnp.int32),
-            dma((8,)), dma((PARTS,)), dma((2, PARTS)), dma((2, PARTS)), dma((2,)), dma((2,)),
+            dma((8,)), dma((PARTS,)), dma((2, STAGES + 1)), dma((2, STAGES + 1)), dma((2,)), dma((2,)),
             dma, dma, dma((7,)), dma((7,)), dma((2, 6)), dma((2, 6)), dma((2, 3)), dma((2, 3)), dma((2, 3)), dma((2, 3)),
             dma((PARTS,)),
         ],

time: 34.8 us -> 31.3 us (0.90)
  Pallas kernels: 32.5 us -> 29 us
    pallas_call x1, Pallas kernels: 32.5 us -> 29 us  [on_device(): pl.pallas_call(kernel, out_shape=jax.ShapeDtypeStruct((RHS, COLS), f32),...]
where the time goes in v3:
time: 31.3 us; the launch traced here: 31.1 us
  Pallas kernels  29 us (93%)
  local copies, waits for them, and re-layouts  2.06 us (7%)
    pallas_call x1, Pallas kernels, on_device(): pl.pallas_call(kernel, out_shape=jax.ShapeDtypeStruct((RHS, COLS), f32),...  29 us
    unnamed x1, local copies, waits for them, and re-layouts  2.06 us

profile of v3, /device:TPU:0, one launch (start us, length us, event | category | flops | bytes accessed | tf_op | source)
XLA Modules:
  0.0 31.1 jit_solution(5738906763266688513)
XLA Ops:
  0.0 29.0 %shard_map.136 = f32[32,6144]{1,0:T(8,128)} custom-call(s32[6,24]{1,0:T(8,128)} %bitcast.2, s32[1,24]{1,0:T(1,128)} %leaf_parent.1, s32[4,6]{1,0:T(4,128)} %bitcast.3, s32[4,8]{1,0:T(4,128)} %node_pairs.1, s32[1,4]{1,0:T(1,128)} %branch_pairs.1, bf16[32,6144]{1,0:T(8,128)(2,1)} %rhs.1, bf16[24,6,256,256]{3,2,1,0:T(8,128)(2,1)} %blocks.1, ...), custom_call_target="tpu_custom_call" | custom-call | flops 1000000000 | bytes 24000000 | tf_op jit(solution)/shard_map/pallas_call | solution.py:400
  29.0 2.1 %copy.16 = f32[32,6144]{1,0:T(8,128)} copy(f32[32,6144]{1,0:T(8,128)} %shard_map.136) | data formatting | bytes 1572864

commit v4 on v3

--- a/solution.py
+++ b/solution.py
@@ -66,14 +66,13 @@
 def kernel(
     near_list, leaf_parent, mid_pairs, node_pairs, branch_pairs,
     rhs, blocks, basis, upward, mid_coupling, mid_transfer, node_coupling, node_transfer,
-    branch_coupling, out,
+    branch_coupling, total,
     rhs_buf, window, late, block_buf, basis_buf, up_raw, mid_coupling_raw, mid_transfer_raw,
     node_coupling_raw, transfer_raw, branch_coupling_raw, up_pair, mid_transfer_pair,
     transfer_pair, coupling_pair, raised, mid_window, mid_field, column, line_a, line_b, chosen_a,
-    chosen_b, got_a, got_b, total, peer_nodes, peer_branches, choice,
+    chosen_b, got_a, got_b, peer_nodes, peer_branches, choice,
     load_sem, block_sem, halo_send, halo_recv, mid_send, mid_recv, transfer_send, transfer_recv,
     column_send, column_recv, pair_send, pair_recv, line_send, line_recv, plane_send, plane_recv,
-    out_sem,
 ):
     b, s = lax.axis_index("branch"), lax.axis_index("sub")
     core, z, x = b % 2, (b // 2) % 4, b // 8
@@ -223,8 +222,6 @@
         send(own_mids, mid_window.at[pl.ds(2 * MIDS, MIDS)], mid_send.at[1], mid_recv.at[1], left),
     ]
     to_halo += send_halo(-SECOND)
-    for stage in range(STAGES - 1):
-        to_halo += send_halo(stage)
 
     def near_self(part):
         block_loads[part].wait()
@@ -243,6 +240,8 @@
         transfer_pair[(1 - core) * 4 + sub] = pair_of(transfer_raw[1 - core, sub])
     for copy in to_column:
         copy.wait_recv()
+    for stage in range(STAGES - 1):
+        to_halo += send_halo(stage)
     for half in range(2):
         top = jnp.zeros((RHS, 128), f32)
         for sub in range(4):
@@ -311,6 +310,15 @@
     for k in range(8):
         coupling_pair[4 + k] = pair_of(node_coupling_raw[k])
 
+    for copy in to_mids:
+        copy.wait_recv()
+    for q in range(MIDS):
+        field = jnp.zeros((RHS, 128), f32)
+        for k in range(4):
+            at = place_of(mid_pairs[k, q], me * MIDS - MIDS, 3 * MIDS)
+            field = field + apply_nt(mid_window[at], pair_of(mid_coupling_raw[q, k]))
+        mid_field[q] = field
+
     for stage in range(BESIDE_LINE):
         near_others(stage)
 
@@ -335,15 +343,6 @@
         got_a[z * SLOTS + k] = line_a[at_x * ITEMS + item]
         got_b[x * SLOTS + k] = line_b[at_z * ITEMS + item]
 
-    for copy in to_mids:
-        copy.wait_recv()
-    for q in range(MIDS):
-        field = jnp.zeros((RHS, 128), f32)
-        for k in range(4):
-            at = place_of(mid_pairs[k, q], me * MIDS - MIDS, 3 * MIDS)
-            field = field + apply_nt(mid_window[at], pair_of(mid_coupling_raw[q, k]))
-        mid_field[q] = field
-
     for stage in range(BESIDE_LINE, STAGES):
         near_others(stage)
 
@@ -371,7 +370,6 @@
     for q in range(MIDS):
         mid_window[q] = split(mid_field[q] + apply_nt(node_field, mid_transfer_pair[q]))
 
-    out_copies = []
     for part in range(PARTS):
         group = range(part * per, part * per + per)
         fields = [split(apply_nt(mid_window[leaf_parent[0, leaf]], up_pair[leaf])) for leaf in group]
@@ -379,12 +377,6 @@
             own = basis_buf[leaf]
             far = nn(field, jnp.concatenate([own, own], axis=0))
             total[:, leaf * LEAF : (leaf + 1) * LEAF] += far
-        at = pl.ds(part * per * LEAF, per * LEAF)
-        copy = pltpu.make_async_copy(total.at[:, at], out.at[:, at], out_sem.at[part])
-        copy.start()
-        out_copies.append(copy)
-    for copy in out_copies:
-        copy.wait()
     for copy in [to_core] + to_column + to_choose + to_mids + to_halo + to_lines + to_planes:
         copy.wait_send()
 
@@ -399,9 +391,9 @@
     hbm = pl.BlockSpec(memory_space=pltpu.HBM)
     return pl.pallas_call(
         kernel,
-        out_shape=jax.ShapeDtypeStruct((RHS, COLS), f32),
+        out_shape=pltpu.VMEM((RHS, COLS), f32),
         in_specs=[smem] * 5 + [hbm] * 9,
-        out_specs=hbm,
+        out_specs=pl.BlockSpec(memory_space=pltpu.VMEM),
         scratch_shapes=[
             pltpu.VMEM((RHS, COLS), bf16),
             pltpu.VMEM((3 * LEAVES + 1, RHS, LEAF), bf16),
@@ -428,16 +420,14 @@
             pltpu.VMEM((3 * SLOTS, 16, 128), bf16),
             pltpu.VMEM((4 * SLOTS + 1, 16, 128), bf16),
             pltpu.VMEM((4 * SLOTS + 1, 16, 128), bf16),
-            pltpu.VMEM((RHS, COLS), f32),
             pltpu.SMEM((6, 4, 8), jnp.int32),
             pltpu.SMEM((6, 1, 4), jnp.int32),
             pltpu.SMEM((6 * SLOTS,), jnp.int32),
             dma((8,)), dma((PARTS,)), dma((2, STAGES + 1)), dma((2, STAGES + 1)), dma((2,)), dma((2,)),
             dma, dma, dma((7,)), dma((7,)), dma((2, 6)), dma((2, 6)), dma((2, 3)), dma((2, 3)), dma((2, 3)), dma((2, 3)),
-            dma((PARTS,)),
         ],
         compiler_params=pltpu.CompilerParams(
-            collective_id=0, has_side_effects=True, vmem_limit_bytes=62 * 2**20
+            collective_id=0, has_side_effects=True, vmem_limit_bytes=58 * 2**20
         ),
         cost_estimate=pl.CostEstimate(
             flops=10**9, bytes_accessed=24 * 10**6, transcendentals=0

time: 31.3 us -> 28.9 us (0.923)
  Pallas kernels: 29 us -> 27.6 us
  local copies, waits for them, and re-layouts: 2.06 us -> 0.88 us
    pallas_call x1, Pallas kernels: 29 us -> 27.6 us  [on_device(): pl.pallas_call(kernel, out_shape=pltpu.VMEM((RHS, COLS), f32), in_specs=[...]
    unnamed x1, local copies, waits for them, and re-layouts: 2.06 us -> 0.88 us
where the time goes in v4:
time: 28.9 us; the launch traced here: 28.5 us
  Pallas kernels  27.6 us (96%)
  local copies, waits for them, and re-layouts  0.88 us (3%)
    pallas_call x1, Pallas kernels, on_device(): pl.pallas_call(kernel, out_shape=pltpu.VMEM((RHS, COLS), f32), in_specs=[...  27.6 us
    unnamed x1, local copies, waits for them, and re-layouts  0.88 us

profile of v4, /device:TPU:0, one launch (start us, length us, event | category | flops | bytes accessed | tf_op | source)
XLA Modules:
  0.0 28.5 jit_solution(13792886104099595366)
XLA Ops:
  0.0 27.6 %shard_map.136 = f32[32,6144]{1,0:T(8,128)S(1)} custom-call(s32[6,24]{1,0:T(8,128)} %bitcast.2, s32[1,24]{1,0:T(1,128)} %leaf_parent.1, s32[4,6]{1,0:T(4,128)} %bitcast.3, s32[4,8]{1,0:T(4,128)} %node_pairs.1, s32[1,4]{1,0:T(1,128)} %branch_pairs.1, bf16[32,6144]{1,0:T(8,128)(2,1)} %rhs.1, bf16[24,6,256,256]{3,2,1,0:T(8,128)(2,1)} %blocks.1, ...), custom_call_target="tpu_custom_call" | custom-call | flops 1000000000 | bytes 24000000 | tf_op jit(solution)/shard_map/pallas_call | solution.py:392
  27.6 0.9 %copy.16 = f32[32,6144]{1,0:T(8,128)} copy(f32[32,6144]{1,0:T(8,128)S(1)} %shard_map.136) | data formatting | bytes 1572864

commit v5 on v4

--- a/solution.py
+++ b/solution.py
@@ -84,7 +84,7 @@
 
     right, left = device((me + 1) % 128), device((me + 127) % 128)
     column_peers = []
-    for d in range(1, 8):
+    for d in (2, 6, 1, 3, 5, 7, 4):
         at = (place + d) % 8
         column_peers.append((x * 8 + z * 2 + at // 4, at % 4))
     x_peers = [(((x + d) % 4) * 8 + z * 2 + core, s) for d in (1, 2, 3)]
@@ -136,6 +136,14 @@
     def columns_of(leaf):
         return pl.ds(pl.multiple_of(leaf * LEAF, LEAF), LEAF)
 
+    parents = [leaf_parent[0, leaf] for leaf in range(LEAVES)]
+    ends = [0]
+    for q in range(1, MIDS):
+        below = 0
+        for parent in parents:
+            below = below + jnp.minimum(jnp.maximum(q - parent, 0), 1)
+        ends.append(below)
+    ends.append(LEAVES)
     for copy in loads[:3]:
         copy.wait()
     for copy in loads[3:] + block_loads:
@@ -173,14 +181,6 @@
     pl.semaphore_wait(barrier, len(peers))
     to_halo = send_halo(SECOND - FIRST)
 
-    parents = [leaf_parent[0, leaf] for leaf in range(LEAVES)]
-    ends = [0]
-    for q in range(1, MIDS):
-        below = 0
-        for parent in parents:
-            below = below + jnp.minimum(jnp.maximum(q - parent, 0), 1)
-        ends.append(below)
-    ends.append(LEAVES)
     mids = []
     for q in range(MIDS):
         value = raised[ends[q]]
@@ -255,13 +255,14 @@
         line_a[x * ITEMS + item] = value[:16]
         line_b[z * ITEMS + item] = value[16:]
     own_a, own_b = line_a.at[pl.ds(x * ITEMS, ITEMS)], line_b.at[pl.ds(z * ITEMS, ITEMS)]
-    to_lines = [
-        send(own_a, own_a, line_send.at[0, d], line_recv.at[0, d], peer)
-        for d, peer in enumerate(x_peers)
-    ] + [
-        send(own_b, own_b, line_send.at[1, d], line_recv.at[1, d], peer)
-        for d, peer in enumerate(z_peers)
-    ]
+    to_lines = []
+    for d in (1, 0, 2):
+        to_lines.append(
+            send(own_a, own_a, line_send.at[0, d], line_recv.at[0, d], x_peers[d])
+        )
+        to_lines.append(
+            send(own_b, own_b, line_send.at[1, d], line_recv.at[1, d], z_peers[d])
+        )
 
     def near_others(stage):
         for copy in to_halo[2 * stage + 2 : 2 * stage + 4] if stage else to_halo[:4]:
@@ -325,7 +326,7 @@
     for copy in to_lines:
         copy.wait_recv()
     to_planes = []
-    for d in range(3):
+    for d in (1, 0, 2):
         for k in range(SLOTS):
             chosen_a[d * SLOTS + k] = line_a[choice[(2 - d) * SLOTS + k]]
             chosen_b[d * SLOTS + k] = line_b[choice[(5 - d) * SLOTS + k]]

time: 28.9 us -> 28.4 us (0.983)
  no operation moved by 1% of the time
where the time goes in v5:
time: 28.4 us; the launch traced here: 28.3 us
  Pallas kernels  27.4 us (96%)
  local copies, waits for them, and re-layouts  0.88 us (3%)
    pallas_call x1, Pallas kernels, on_device(): pl.pallas_call(kernel, out_shape=pltpu.VMEM((RHS, COLS), f32), in_specs=[...  27.4 us
    unnamed x1, local copies, waits for them, and re-layouts  0.88 us

profile of v5, /device:TPU:0, one launch (start us, length us, event | category | flops | bytes accessed | tf_op | source)
XLA Modules:
  0.0 28.3 jit_solution(12431817804629366051)
XLA Ops:
  0.0 27.4 %shard_map.136 = f32[32,6144]{1,0:T(8,128)S(1)} custom-call(s32[6,24]{1,0:T(8,128)} %bitcast.2, s32[1,24]{1,0:T(1,128)} %leaf_parent.1, s32[4,6]{1,0:T(4,128)} %bitcast.3, s32[4,8]{1,0:T(4,128)} %node_pairs.1, s32[1,4]{1,0:T(1,128)} %branch_pairs.1, bf16[32,6144]{1,0:T(8,128)(2,1)} %rhs.1, bf16[24,6,256,256]{3,2,1,0:T(8,128)(2,1)} %blocks.1, ...), custom_call_target="tpu_custom_call" | custom-call | flops 1000000000 | bytes 24000000 | tf_op jit(solution)/shard_map/pallas_call | solution.py:393
  27.4 0.9 %copy.16 = f32[32,6144]{1,0:T(8,128)} copy(f32[32,6144]{1,0:T(8,128)S(1)} %shard_map.136) | data formatting | bytes 1572864

commit v6 on v5

--- a/solution.py
+++ b/solution.py
@@ -323,20 +323,23 @@
     for stage in range(BESIDE_LINE):
         near_others(stage)
 
-    for copy in to_lines:
-        copy.wait_recv()
     to_planes = []
+    for copy in to_lines[0::2]:
+        copy.wait_recv()
     for d in (1, 0, 2):
         for k in range(SLOTS):
             chosen_a[d * SLOTS + k] = line_a[choice[(2 - d) * SLOTS + k]]
+        to_planes.append(
+            send(chosen_a.at[pl.ds(d * SLOTS, SLOTS)], got_a.at[pl.ds(z * SLOTS, SLOTS)],
+                 plane_send.at[0, d], plane_recv.at[0, d], z_peers[d])
+        )
+    for copy in to_lines[1::2]:
+        copy.wait_recv()
+    for d in (1, 0, 2):
+        for k in range(SLOTS):
             chosen_b[d * SLOTS + k] = line_b[choice[(5 - d) * SLOTS + k]]
-        at = pl.ds(d * SLOTS, SLOTS)
         to_planes.append(
-            send(chosen_a.at[at], got_a.at[pl.ds(z * SLOTS, SLOTS)],
-                 plane_send.at[0, d], plane_recv.at[0, d], z_peers[d])
-        )
-        to_planes.append(
-            send(chosen_b.at[at], got_b.at[pl.ds(x * SLOTS, SLOTS)],
+            send(chosen_b.at[pl.ds(d * SLOTS, SLOTS)], got_b.at[pl.ds(x * SLOTS, SLOTS)],
                  plane_send.at[1, d], plane_recv.at[1, d], x_peers[d])
         )
     for k in range(SLOTS):

time: 28.4 us -> 28.4 us (level)
  no operation moved by 1% of the time
where the time goes in v6:
time: 28.4 us; the launch traced here: 28.2 us
  Pallas kernels  27.3 us (96%)
  local copies, waits for them, and re-layouts  0.88 us (3%)
    pallas_call x1, Pallas kernels, on_device(): pl.pallas_call(kernel, out_shape=pltpu.VMEM((RHS, COLS), f32), in_specs=[...  27.3 us
    unnamed x1, local copies, waits for them, and re-layouts  0.88 us

profile of v6, /device:TPU:0, one launch (start us, length us, event | category | flops | bytes accessed | tf_op | source)
XLA Modules:
  0.0 28.2 jit_solution(13250478921127315706)
XLA Ops:
  0.0 27.3 %shard_map.136 = f32[32,6144]{1,0:T(8,128)S(1)} custom-call(s32[6,24]{1,0:T(8,128)} %bitcast.2, s32[1,24]{1,0:T(1,128)} %leaf_parent.1, s32[4,6]{1,0:T(4,128)} %bitcast.3, s32[4,8]{1,0:T(4,128)} %node_pairs.1, s32[1,4]{1,0:T(1,128)} %branch_pairs.1, bf16[32,6144]{1,0:T(8,128)(2,1)} %rhs.1, bf16[24,6,256,256]{3,2,1,0:T(8,128)(2,1)} %blocks.1, ...), custom_call_target="tpu_custom_call" | custom-call | flops 1000000000 | bytes 24000000 | tf_op jit(solution)/shard_map/pallas_call | solution.py:396
  27.3 0.9 %copy.16 = f32[32,6144]{1,0:T(8,128)} copy(f32[32,6144]{1,0:T(8,128)S(1)} %shard_map.136) | data formatting | bytes 1572864
